TPU v7x, 32 devices: a whole 2x2x4 slice. The times are simulated.
32 devices in a mesh: pairs: 8 (over y, x, core), band: 4 (over z).
Axes of the slice: x: 2, y: 2, z: 4, core: 2. Of those that a mesh axis runs over, the one named last changes fastest.
Arguments:
- spectra: bfloat16 [4096, 4, 1024], P('pairs', 'band'), may hold values from -15 to 15
- observed: bfloat16 [16384, 4, 1024], P('pairs', 'band'), may hold values from -5 to 5
- pair_owner: int32 [16384, 2], P('pairs'), may hold values from 0 to 7, all different within a row; in each aligned block of 2048 rows (0 to 2047, 2048 to 4095, ...) at most 768 rows name the same one
- pair_slot: int32 [16384, 2], P('pairs'), may hold values from 0 to 511
- win_start: int32 [16384], P('pairs'), may hold values from 0 to 511
- win_end: int32 [16384], P('pairs'), may hold values from 513 to 1024
Outputs:
- noise_kernel: float32 [4096, 4, 512], P('pairs', 'band')
Inputs may be any that keep to these rules, and one draw needn't show every extreme that they name: `pair_owner`: the two stations of a pair have different owners; among the pairs of one index of pairs no owner is named more than 768 times, a bound that some block reaches.
All inputs are finite; a program needn't handle non-finite values.
Results may differ from a plain program's by a relative error of at most 0.006.
Values may be sent and summed in bfloat16 or wider, within the bound.
A program may use at most 128 MiB of HBM per device.

v0:
```python
import math

import jax
import jax.numpy as jnp
from jax import lax
from jax.sharding import PartitionSpec as P


def lag_basis(half_width, lag_count):
    freqs = jnp.arange(half_width, dtype=jnp.int32)
    lag_index = jnp.arange(lag_count, dtype=jnp.int32)
    phases = (freqs[:, None] * lag_index[None, :] % lag_count).astype(jnp.float32) * (
        2.0 * math.pi / lag_count
    )
    factor = 1.0 / math.sqrt(lag_count)
    return jnp.concatenate([jnp.cos(phases) * factor, -jnp.sin(phases) * factor], axis=0).astype(
        jnp.bfloat16
    )


def owner_positions(owner_flat, owner_count):
    onehot = (owner_flat[:, None] == jnp.arange(owner_count, dtype=jnp.int32)[None, :]).astype(
        jnp.int32
    )
    before = jnp.cumsum(onehot, axis=0) - onehot
    return jnp.sum(before * onehot, axis=1)


def shards(spectra, observed, pair_owner, pair_slot, win_start, win_end):
    owners = lax.axis_size("pairs")
    station_count = spectra.shape[0]
    band_count = spectra.shape[1]
    full_width = spectra.shape[2]
    half_width = full_width // 2
    pair_count = observed.shape[0]
    lag_count = observed.shape[2]
    capacity = 3 * pair_count // owners
    spectrum = spectra.astype(jnp.float32)
    local_power = jnp.sum(spectrum * spectrum, axis=(1, 2))
    total_power = lax.psum(local_power, "band")
    entries = band_count * lax.axis_size("band") * full_width
    whitened = (spectrum * lax.rsqrt(total_power / entries + 1e-05)[:, None, None]).astype(
        jnp.bfloat16
    )
    owner_flat = pair_owner.reshape(-1)
    slot_flat = pair_slot.reshape(-1)
    position = owner_positions(owner_flat, owners)
    request = (
        jnp.full((owners, capacity), station_count, jnp.int32)
        .at[owner_flat, position]
        .set(slot_flat)
    )
    wanted = lax.all_to_all(request, "pairs", split_axis=0, concat_axis=0, tiled=True)
    panel_rows = lax.all_gather(whitened, "pairs", axis=0, tiled=True)
    fetched = panel_rows[owner_flat * station_count + slot_flat]
    fetched = fetched.reshape(pair_count, 2, band_count, full_width)
    near_end = fetched[:, 0].astype(jnp.float32)
    far_end = fetched[:, 1].astype(jnp.float32)
    near_re, near_im = (near_end[..., :half_width], near_end[..., half_width:])
    far_re, far_im = (far_end[..., :half_width], far_end[..., half_width:])
    cross_spec = jnp.concatenate(
        [near_re * far_re + near_im * far_im, near_im * far_re - near_re * far_im], axis=-1
    ).astype(jnp.bfloat16)
    table = lag_basis(half_width, lag_count)
    lagged = jnp.einsum("pbf,ft->pbt", cross_spec, table, preferred_element_type=jnp.float32)
    lag_index = jnp.arange(lag_count, dtype=jnp.int32)
    window = (
        (lag_index[None, :] >= win_start[:, None]) & (lag_index[None, :] < win_end[:, None])
    ).astype(jnp.float32)
    residual = (window[:, None, :] * (lagged - observed.astype(jnp.float32))).astype(jnp.bfloat16)
    adjoint = jnp.einsum("pbt,ft->pbf", residual, table, preferred_element_type=jnp.float32)
    adj_re, adj_im = (adjoint[..., :half_width], adjoint[..., half_width:])
    to_first = jnp.concatenate(
        [adj_re * far_re - adj_im * far_im, adj_re * far_im + adj_im * far_re], axis=-1
    ).astype(jnp.bfloat16)
    to_second = jnp.concatenate(
        [adj_re * near_re + adj_im * near_im, adj_re * near_im - adj_im * near_re], axis=-1
    ).astype(jnp.bfloat16)
    stacked = jnp.stack([to_first, to_second], axis=1).reshape(
        2 * pair_count, band_count, full_width
    )
    outgoing = (
        jnp.zeros((owners, capacity, band_count, full_width), jnp.bfloat16)
        .at[owner_flat, position]
        .set(stacked)
    )
    incoming = lax.all_to_all(outgoing, "pairs", split_axis=0, concat_axis=0, tiled=True)

    def add_source(source, summed):
        block_rows = lax.dynamic_index_in_dim(incoming, source, 0, keepdims=False).astype(
            jnp.float32
        )
        block_ids = lax.dynamic_index_in_dim(wanted, source, 0, keepdims=False)
        return summed.at[block_ids].add(block_rows)

    summed = lax.fori_loop(
        0, owners, add_source, jnp.zeros((station_count + 1, band_count, full_width), jnp.float32)
    )
    summed = summed[:station_count]
    own_spec = whitened.astype(jnp.float32)
    return 0.25 * (
        summed[..., :half_width] * own_spec[..., :half_width]
        + summed[..., half_width:] * own_spec[..., half_width:]
    )


def solution(mesh):
    return jax.shard_map(
        shards,
        mesh=mesh,
        in_specs=(
            P("pairs", "band", None),
            P("pairs", "band", None),
            P("pairs", None),
            P("pairs", None),
            P("pairs"),
            P("pairs"),
        ),
        out_specs=P("pairs", "band", None),
        check_vma=False,
    )
```

profile of v0, /device:TPU:0, one launch (start us, length us, event | category | flops | bytes accessed | tf_op | source)
XLA Modules:
  0.0 521.2 jit_solution(8301477645746704293)
XLA Ops:
  8.1 13.5 %psum.7 = f32[512]{0:T(512)S(1)} all-reduce(f32[512]{0:T(512)S(1)} %fusion.14), channel_id=1, replica_groups=mesh['pairs'=8,'band'=4] {'band'}, use_global_device_ids=true, to_apply=%region_4.5 | all-reduce | flops 512 | bytes 4096 | tf_op jit(solution)/shard_map/psum | solution.py:40
  21.5 3.2 fusion.43
  28.2 2.3 reduce-window.6
  31.6 16.1 %scatter_custom_fusion.1 = s32[6144]{0:T(1024)} fusion(s32[4096]{0:T(1024)S(1)} %broadcast_select_fusion, s32[4096]{0:T(1024)S(1)} %reshape.381, s32[]{:T(128)} %constant.75.clone.1), kind=kCustom, calls=%fused_computation.74 | custom fusion | bytes 24580
  47.7 4.3 all-to-all-start
  52.0 9.2 %multiply_convert_fusion = (bf16[512,1024]{1,0:T(8,128)(2,1)S(1)}, bf16[512,1024]{1,0:T(8,128)(2,1)}) fusion(), kind=kLoop, calls=%fused_computation.49 | loop fusion | flops 9961472 | bytes 2097152 | tf_op jit(solution)/shard_map/convert.12
  61.2 16.6 %all-gather.2.cloned.1.call-done = bf16[4096,1,1024]{2,0,1:T(8,128)(2,1)} async-done(((bf16[512,1,1024]{2,0,1:T(8,128)(2,1)}), bf16[4096,1,1024]{2,0,1:T(8,128)(2,1)}) %all-gather.2.cloned.1.call-update) | async-done | bytes 8388624 | tf_op jit(solution)/shard_map/all_gather | solution.py:54
  77.8 25.4 %gather_fusion = bf16[4096,1024]{1,0:T(8,128)(2,1)} fusion(bf16[4096,1024]{1,0:T(8,128)(2,1)} %bitcast.80, s32[4096]{0:T(1024)S(1)} %broadcast_clamp_fusion), kind=kCustom, calls=%fused_computation | custom fusion | bytes 16793600 | tf_op jit(solution)/shard_map/gather | solution.py:55
  103.2 13.1 %reshape.340 = bf16[2048,2,1,1024]{3,1,0,2:T(2,128)(2,1)} reshape(bf16[4096,1024]{1,0:T(8,128)(2,1)} %gather_fusion) | data formatting | bytes 16777216 | tf_op jit(solution)/shard_map/reshape | solution.py:56
  116.3 17.2 %fusion.45 = (bf16[2048,1,1,1024]{3,1,0,2:T(2,128)(2,1)}, bf16[2048,1,1,1024]{3,1,0,2:T(2,128)(2,1)}) fusion(bf16[2048,2,1,1024]{3,1,0,2:T(2,128)(2,1)} %reshape.340), kind=kLoop, calls=%fused_computation.82 | loop fusion | bytes 16777216 | tf_op jit(solution)/shard_map/slice | solution.py:58
  133.5 20.1 %copy.28 = bf16[2048,1,1,1024]{0,3,2,1:T(8,128)(2,1)} copy(bf16[2048,1,1,1024]{3,1,0,2:T(2,128)(2,1)} %get-tuple-element.103) | data formatting | bytes 8388608
  153.6 6.7 %bitcast_convert_fusion = f32[2048,1,1024]{0,2,1:T(8,128)} fusion(bf16[2048,1,1,1024]{0,3,2,1:T(8,128)(2,1)} %copy.28), kind=kLoop, calls=%fused_computation.24 | loop fusion | flops 2097152 | bytes 12582912 | tf_op jit(solution)/shard_map/convert_element_type | solution.py:58
  160.3 20.0 %copy.27 = bf16[2048,1,1,1024]{0,3,2,1:T(8,128)(2,1)} copy(bf16[2048,1,1,1024]{3,1,0,2:T(2,128)(2,1)} %get-tuple-element.104) | data formatting | bytes 8388608
  180.3 3.4 bitcast_convert_fusion.1
  184.9 4.2 fusion.19
  189.2 16.3 %convolution_bitcast_fusion = f32[2048,1,1024]{0,2,1:T(8,128)} fusion(bf16[2048,1,1024]{2,0,1:T(8,128)(2,1)} %param.9, bf16[2048,512]{0,1:T(8,128)(2,1)} %get-tuple-element.100, bf16[2048,512]{0,1:T(8,128)(2,1)S(1)} %get-tuple-element.99, s32[2048]{0:T(1024)S(1)} %copy-done.6, s32[2048]{0:T(1024)S(1)} %copy-done.7, ...), kind=kOutput, calls=%fused_computation.19 | convolution fusion | flops 8621391872 | bytes 18890752 | tf_op jit(solution)/shard_map/pbt,ft->pbf/dot_general | solution.py:71
  205.5 10.1 %fusion.21 = (bf16[2048,1,1,512]{0,3,2,1:T(8,128)(2,1)S(1)}, bf16[2048,1,1,512]{0,3,2,1:T(8,128)(2,1)S(1)}, bf16[2048,1,1,512]{0,3,2,1:T(8,128)(2,1)S(1)}, bf16[2048,1,1,512]{0,3,2,1:T(8,128)(2,1)S(1)}) fusion(f32[2048,1,1024]{0,2,1:T(8,128)} %bitcast_convert_fusion, f32[2048,1,1024]{0,2,1:T(8,128)} %convolution_bitcast_fusion, f32[2048,1,1024]{0,2,1:T(8,128)} %copy-done.1), kind=kLoop, calls=%fused_computation.44 | loop fusion | flops 16777216 | bytes 33554432 | tf_op jit(solution)/shard_map/concatenate | solution.py:73
  215.6 4.0 maximum_maximum_fusion
  219.7 21.4 %copy.24 = bf16[2048,2,1,1024]{3,1,0,2:T(2,128)(2,1)} copy(bf16[2048,2,1,1024]{0,3,2,1:T(8,128)(2,1)} %maximum_maximum_fusion) | data formatting | bytes 16777216 | tf_op jit(solution)/shard_map/stack | solution.py:79
  241.0 13.3 %reshape.391 = bf16[4096,1024]{1,0:T(8,128)(2,1)} reshape(bf16[2048,2,1,1024]{3,1,0,2:T(2,128)(2,1)} %copy.24) | data formatting | bytes 16777216 | tf_op jit(solution)/shard_map/reshape | solution.py:79
  254.3 26.5 %scatter_custom_fusion.2 = bf16[6144,1024]{1,0:T(8,128)(2,1)} fusion(s32[4096]{0:T(1024)S(1)} %broadcast_select_fusion, bf16[4096,1024]{1,0:T(8,128)(2,1)} %reshape.391, bf16[]{:T(256)} %constant.70.clone.1), kind=kCustom, calls=%fused_computation.17 | custom fusion | bytes 12583424
  280.9 5.6 %all-to-all-start.1 = ((bf16[8,768,1,1024]{3,1,2,0:T(8,128)(2,1)}), bf16[8,768,1,1024]{3,1,2,0:T(8,128)(2,1)}, u32[]{:S(2)}, u32[]{:S(2)}) async-start(bf16[8,768,1,1024]{3,1,2,0:T(8,128)(2,1)} %bitcast.81), calls=%async_computation.1 | async-start | bytes 25165824 | tf_op jit(solution)/shard_map/all_to_all | solution.py:87
  286.5 139.0 %all-to-all-done.1 = bf16[8,768,1,1024]{3,1,2,0:T(8,128)(2,1)} async-done(((bf16[8,768,1,1024]{3,1,2,0:T(8,128)(2,1)}), bf16[8,768,1,1024]{3,1,2,0:T(8,128)(2,1)}, u32[]{:S(2)}, u32[]{:S(2)}) %all-to-all-start.1) | async-done | bytes 12582944 | tf_op jit(solution)/shard_map/all_to_all | solution.py:87
  425.7 84.3 %while.13 = (s32[]{:T(128)}, f32[513,1,1024]{2,0,1:T(8,128)S(1)}, s32[8,768]{1,0:T(8,128)S(1)}, bf16[8,768,1,1024]{3,1,2,0:T(8,128)(2,1)}, s32[]{:T(128)}, /*index=5*/s32[]{:T(128)}) while((s32[]{:T(128)}, f32[513,1,1024]{2,0,1:T(8,128)S(1)}, s32[8,768]{1,0:T(8,128)S(1)}, bf16[8,768,1,1024]{3,1,2,0:T(8,128)(2,1)}, s32[]{:T(128)}, ...), condition=%wide.region_9.10_spmd, body=%wide.region_7.9_spmd.sunk | while | flops 1575170 | bytes 3681353 | solution.py:96
  425.8 10.5 %scatter_custom_fusion.9 = f32[513,1024]{1,0:T(8,128)S(1)} fusion(f32[513,1024]{1,0:T(8,128)S(1)} %bitcast.82, s32[768]{0:T(1024)S(1)} %fusion.49, bf16[8,768,1,1024]{3,1,2,0:T(8,128)(2,1)} %get-tuple-element.150, s32[]{:T(128)} %get-tuple-element.141, s32[]{:T(128)} %constant.68.clone.1..sunk), kind=kCustom, calls=%fused_computation.4.clone.1 | custom fusion | flops 1572864 | bytes 3675136 | tf_op jit(solution)/shard_map/while/body/eval_jaxpr/scatter-add | solution.py:94
  436.3 10.5 %scatter_custom_fusion.9 = f32[513,1024]{1,0:T(8,128)S(1)} fusion(f32[513,1024]{1,0:T(8,128)S(1)} %bitcast.82, s32[768]{0:T(1024)S(1)} %fusion.49, bf16[8,768,1,1024]{3,1,2,0:T(8,128)(2,1)} %get-tuple-element.150, s32[]{:T(128)} %get-tuple-element.141, s32[]{:T(128)} %constant.68.clone.1..sunk), kind=kCustom, calls=%fused_computation.4.clone.1 | custom fusion | flops 1572864 | bytes 3675136 | tf_op jit(solution)/shard_map/while/body/eval_jaxpr/scatter-add | solution.py:94
  446.8 10.5 %scatter_custom_fusion.9 = f32[513,1024]{1,0:T(8,128)S(1)} fusion(f32[513,1024]{1,0:T(8,128)S(1)} %bitcast.82, s32[768]{0:T(1024)S(1)} %fusion.49, bf16[8,768,1,1024]{3,1,2,0:T(8,128)(2,1)} %get-tuple-element.150, s32[]{:T(128)} %get-tuple-element.141, s32[]{:T(128)} %constant.68.clone.1..sunk), kind=kCustom, calls=%fused_computation.4.clone.1 | custom fusion | flops 1572864 | bytes 3675136 | tf_op jit(solution)/shard_map/while/body/eval_jaxpr/scatter-add | solution.py:94
  457.4 10.5 %scatter_custom_fusion.9 = f32[513,1024]{1,0:T(8,128)S(1)} fusion(f32[513,1024]{1,0:T(8,128)S(1)} %bitcast.82, s32[768]{0:T(1024)S(1)} %fusion.49, bf16[8,768,1,1024]{3,1,2,0:T(8,128)(2,1)} %get-tuple-element.150, s32[]{:T(128)} %get-tuple-element.141, s32[]{:T(128)} %constant.68.clone.1..sunk), kind=kCustom, calls=%fused_computation.4.clone.1 | custom fusion | flops 1572864 | bytes 3675136 | tf_op jit(solution)/shard_map/while/body/eval_jaxpr/scatter-add | solution.py:94
  467.9 10.5 %scatter_custom_fusion.9 = f32[513,1024]{1,0:T(8,128)S(1)} fusion(f32[513,1024]{1,0:T(8,128)S(1)} %bitcast.82, s32[768]{0:T(1024)S(1)} %fusion.49, bf16[8,768,1,1024]{3,1,2,0:T(8,128)(2,1)} %get-tuple-element.150, s32[]{:T(128)} %get-tuple-element.141, s32[]{:T(128)} %constant.68.clone.1..sunk), kind=kCustom, calls=%fused_computation.4.clone.1 | custom fusion | flops 1572864 | bytes 3675136 | tf_op jit(solution)/shard_map/while/body/eval_jaxpr/scatter-add | solution.py:94
  478.4 10.5 %scatter_custom_fusion.9 = f32[513,1024]{1,0:T(8,128)S(1)} fusion(f32[513,1024]{1,0:T(8,128)S(1)} %bitcast.82, s32[768]{0:T(1024)S(1)} %fusion.49, bf16[8,768,1,1024]{3,1,2,0:T(8,128)(2,1)} %get-tuple-element.150, s32[]{:T(128)} %get-tuple-element.141, s32[]{:T(128)} %constant.68.clone.1..sunk), kind=kCustom, calls=%fused_computation.4.clone.1 | custom fusion | flops 1572864 | bytes 3675136 | tf_op jit(solution)/shard_map/while/body/eval_jaxpr/scatter-add | solution.py:94
  489.0 10.5 %scatter_custom_fusion.9 = f32[513,1024]{1,0:T(8,128)S(1)} fusion(f32[513,1024]{1,0:T(8,128)S(1)} %bitcast.82, s32[768]{0:T(1024)S(1)} %fusion.49, bf16[8,768,1,1024]{3,1,2,0:T(8,128)(2,1)} %get-tuple-element.150, s32[]{:T(128)} %get-tuple-element.141, s32[]{:T(128)} %constant.68.clone.1..sunk), kind=kCustom, calls=%fused_computation.4.clone.1 | custom fusion | flops 1572864 | bytes 3675136 | tf_op jit(solution)/shard_map/while/body/eval_jaxpr/scatter-add | solution.py:94
  499.5 10.5 %scatter_custom_fusion.9 = f32[513,1024]{1,0:T(8,128)S(1)} fusion(f32[513,1024]{1,0:T(8,128)S(1)} %bitcast.82, s32[768]{0:T(1024)S(1)} %fusion.49, bf16[8,768,1,1024]{3,1,2,0:T(8,128)(2,1)} %get-tuple-element.150, s32[]{:T(128)} %get-tuple-element.141, s32[]{:T(128)} %constant.68.clone.1..sunk), kind=kCustom, calls=%fused_computation.4.clone.1 | custom fusion | flops 1572864 | bytes 3675136 | tf_op jit(solution)/shard_map/while/body/eval_jaxpr/scatter-add | solution.py:94
  (50 shorter events, 11.7 us)
Async XLA Ops:
  6.5 18.2 %copy-start.2 = (s32[2048,2]{0,1:T(2,128)S(1)}, s32[2048,2]{0,1:T(2,128)}, u32[]{:S(2)}) copy-start(s32[2048,2]{0,1:T(2,128)} %param.10) | copy-start | bytes 49156
  6.5 71.2 %all-gather.2.cloned.1.call-start = ((), (), s32[]{:S(2)}) async-start(), calls=%async_computation.2 | async-start | bytes 9437184 | tf_op jit(solution)/shard_map/all_gather | solution.py:54
  21.5 5.2 copy-start.3
  24.7 6.6 %copy-start.5 = (s32[2]{0:T(128)S(1)}, s32[2]{0:T(128)}, u32[]{:S(2)}) copy-start(s32[2]{0:T(128)} %constant.84) | copy-start | bytes 28
  24.7 6.7 %copy-start.4 = (s32[2]{0:T(128)S(1)}, s32[2]{0:T(128)}, u32[]{:S(2)}) copy-start(s32[2]{0:T(128)} %constant.87) | copy-start | bytes 28
  47.7 233.2 %all-to-all-start = ((s32[8,1,768]{2,1,0:T(1,128)}), s32[8,1,768]{2,1,0:T(1,128)S(1)}, u32[]{:S(2)}, u32[]{:S(2)}) async-start(s32[8,1,768]{2,1,0:T(1,128)} %bitcast.6), calls=%async_computation | async-start | bytes 49152 | tf_op jit(solution)/shard_map/all_to_all | solution.py:53
  180.3 4.6 copy-start
  184.9 4.2 copy-start.1
  184.9 4.3 copy-start.6
  184.9 4.3 copy-start.7
  280.9 144.6 %all-to-all-start.1 = ((bf16[8,768,1,1024]{3,1,2,0:T(8,128)(2,1)}), bf16[8,768,1,1024]{3,1,2,0:T(8,128)(2,1)}, u32[]{:S(2)}, u32[]{:S(2)}) async-start(bf16[8,768,1,1024]{3,1,2,0:T(8,128)(2,1)} %bitcast.81), calls=%async_computation.1 | async-start | bytes 25165824 | tf_op jit(solution)/shard_map/all_to_all | solution.py:87
Sparse Core Ops, SparseCore 0:
  24.8 52.8 all-gather.1
where the time goes:
time: 529 us; the launch traced here: 521 us
  local copies, waits for them, and re-layouts  180 us (34%)
  waiting for transfers between devices  156 us (29%)
  other arithmetic  131 us (25%)
  matrix products  16.3 us (3%)
  between operations  13.9 us (3%)
  blocking collectives  13.5 us (3%)
  starting transfers between devices  9.87 us (2%)
    all_to_all x1, waiting for transfers between devices, shards(): lax.all_to_all(outgoing, 'pairs', split_axis=0, concat_axis=0, tiled=True)  139 us
    unnamed x23, local copies, waits for them, and re-layouts  84.7 us
    scatter-add x8, other arithmetic, add_source(): return summed.at[block_ids].add(block_rows)  83.9 us
    gather x1, local copies, waits for them, and re-layouts, shards(): fetched = panel_rows[owner_flat * station_count + slot_flat]  25.4 us
    another operation x1, local copies, waits for them, and re-layouts, shards(): jnp.stack([to_first, to_second], axis=1)  21.4 us
    slice x1, local copies, waits for them, and re-layouts, shards(): far_end = fetched[:, 1].astype(jnp.float32)  17.2 us
    all_gather x1, waiting for transfers between devices, shards(): panel_rows = lax.all_gather(whitened, 'pairs', axis=0, tiled=True)  16.6 us
    dot_general x1, matrix products, shards(): jnp.einsum('pbt,ft->pbf', residual, table, preferred_element_type=jnp.flo...  16.3 us
  transfers between devices with their start and end apart: 3, of which 2 were waited for; matrix products, arithmetic and copies ran while one was open for 45% of the time, Pallas kernels for 0%

commit v1 on v0

--- a/solution.py
+++ b/solution.py
@@ -1,9 +1,417 @@
+import functools
 import math
 
 import jax
 import jax.numpy as jnp
+import numpy as np
 from jax import lax
+from jax.experimental import pallas as pl
+from jax.experimental.pallas import tpu as pltpu
 from jax.sharding import PartitionSpec as P
+
+MESH = pl.DeviceIdType.MESH
+VMEM_LIMIT = 60 * 1024 * 1024
+
+
+def basis_constant(half_width, lag_count):
+    phases = (np.arange(half_width)[:, None] * np.arange(lag_count)[None, :] % lag_count) * (
+        2.0 * math.pi / lag_count
+    )
+    factor = 1.0 / math.sqrt(lag_count)
+    table = np.concatenate([np.cos(phases) * factor, -np.sin(phases) * factor], axis=0)
+    return table.astype(np.float32)
+
+
+def neighbours(me):
+    core, x, y = me % 2, (me // 2) % 2, me // 4
+    across, along = me + 2 - 4 * x, me + 4 - 8 * y
+    return across, along, across + 4 - 8 * y, me + 1 - 2 * core
+
+
+def gather_kernel(
+    bands, entries, owners, spec_ref, src_ref, arr_ref, scale_ref,
+    part, part_recv, total, total_recv,
+    local_sem, send_sem, recv_sem, band_send, band_recv, total_send, total_recv_sem,
+):
+    me = lax.axis_index("pairs")
+    band = lax.axis_index("band")
+    across, along, diagonal, sibling = neighbours(me)
+    half = src_ref.shape[0] // 2
+
+    barrier = pltpu.get_barrier_semaphore()
+    for k in range(1, owners):
+        pl.semaphore_signal(
+            barrier, inc=1, device_id={"pairs": lax.rem(me + k, owners)}, device_id_type=MESH
+        )
+    for k in range(1, bands):
+        pl.semaphore_signal(
+            barrier, inc=1, device_id={"band": lax.rem(band + k, bands)}, device_id_type=MESH
+        )
+    pl.semaphore_wait(barrier, owners + bands - 2)
+
+    def rows(part_index):
+        return pl.ds(part_index * half, half)
+
+    def push(src, owner, part_index, sem, target):
+        copy = pltpu.make_async_remote_copy(
+            src_ref=src,
+            dst_ref=arr_ref.at[owner, rows(part_index)],
+            send_sem=send_sem.at[sem[0]],
+            recv_sem=recv_sem.at[sem[1]],
+            device_id={"pairs": target},
+            device_id_type=MESH,
+        )
+        copy.start()
+        return copy
+
+    def arrived(owner, part_index, sem):
+        slot = arr_ref.at[owner, rows(part_index)]
+        pltpu.make_async_remote_copy(
+            src_ref=slot, dst_ref=slot, send_sem=send_sem.at[0], recv_sem=recv_sem.at[sem],
+            device_id={"pairs": me + 1 - 2 * (me % 2)}, device_id_type=MESH,
+        ).wait_recv()
+
+    sent = []
+    own = [src_ref.at[rows(0)], src_ref.at[rows(1)]]
+    sent.append(push(own[0], me, 0, (0, 0), across))
+    sent.append(push(own[1], me, 1, (1, 3), along))
+    sent.append(push(own[1], me, 1, (2, 1), across))
+    sent.append(push(own[0], me, 0, (3, 2), along))
+    sent.append(push(own[0], me, 0, (4, 6), sibling))
+    sent.append(push(own[1], me, 1, (5, 7), sibling))
+    local = pltpu.make_async_copy(src_ref, arr_ref.at[me], local_sem)
+    local.start()
+
+    spectrum = spec_ref[...].astype(jnp.float32)
+    square = spectrum * spectrum
+    high = square.astype(jnp.bfloat16)
+    low = (square - high.astype(jnp.float32)).astype(jnp.bfloat16)
+    ones = jnp.ones((8, spec_ref.shape[1]), jnp.bfloat16)
+    dims = (((1,), (1,)), ((), ()))
+    part[...] = lax.dot_general(
+        ones, high, dims, preferred_element_type=jnp.float32
+    ) + lax.dot_general(ones, low, dims, preferred_element_type=jnp.float32)
+    copies = []
+    for k in range(1, bands):
+        copy = pltpu.make_async_remote_copy(
+            src_ref=part, dst_ref=part_recv.at[k], send_sem=band_send.at[k],
+            recv_sem=band_recv.at[k],
+            device_id={"band": lax.rem(band + k, bands)}, device_id_type=MESH,
+        )
+        copy.start()
+        copies.append(copy)
+    for copy in copies:
+        copy.wait()
+    power = part[...]
+    for k in range(1, bands):
+        power = power + part_recv[k]
+    total[...] = lax.rsqrt(power / entries + 1e-05)
+    copies = []
+    for k in range(1, owners):
+        copy = pltpu.make_async_remote_copy(
+            src_ref=total, dst_ref=total_recv.at[me], send_sem=total_send.at[k],
+            recv_sem=total_recv_sem.at[k],
+            device_id={"pairs": lax.rem(me + k, owners)}, device_id_type=MESH,
+        )
+        copy.start()
+        copies.append(copy)
+
+    arrived(across, 0, 0)
+    sent.append(push(arr_ref.at[across, rows(0)], across, 0, (6, 4), along))
+    sent.append(push(arr_ref.at[across, rows(0)], across, 0, (7, 8), sibling))
+    arrived(along, 1, 3)
+    sent.append(push(arr_ref.at[along, rows(1)], along, 1, (8, 5), across))
+    sent.append(push(arr_ref.at[along, rows(1)], along, 1, (9, 11), sibling))
+    arrived(across, 1, 1)
+    sent.append(push(arr_ref.at[across, rows(1)], across, 1, (10, 9), sibling))
+    arrived(along, 0, 2)
+    sent.append(push(arr_ref.at[along, rows(0)], along, 0, (11, 10), sibling))
+    for k in range(1, owners):
+        copies[k - 1].wait()
+    for o in range(owners):
+        scale_ref[o] = jnp.where(me == o, total[...], total_recv[o])
+    arrived(diagonal, 0, 4)
+    sent.append(push(arr_ref.at[diagonal, rows(0)], diagonal, 0, (12, 12), sibling))
+    arrived(diagonal, 1, 5)
+    sent.append(push(arr_ref.at[diagonal, rows(1)], diagonal, 1, (13, 13), sibling))
+    shift = 1 - 2 * (me % 2)
+    for index, chip in enumerate((me, across, along, diagonal)):
+        arrived(chip + shift, 0, 6 + 2 * index)
+        arrived(chip + shift, 1, 7 + 2 * index)
+    for copy in sent:
+        copy.wait_send()
+    local.wait()
+
+
+def pair_kernel(
+    ids_ref, arr_ref, scale_ref, observed_ref, window_ref, table_ref, back_ref, out_ref,
+    panel, near, far, cross,
+):
+    step = pl.program_id(0)
+    owners, stations, width = arr_ref.shape
+    tile = observed_ref.shape[0]
+    groups = width // 128
+    fold = groups // 2
+    half = width // 2
+    chunk = 64
+
+    @pl.when(step == 0)
+    def _():
+        def whiten(o, carry):
+            scale = scale_ref[o].T[:, 0:1]
+            for r in range(0, stations, chunk):
+                rows = arr_ref[o, r : r + chunk, :].astype(jnp.float32) * scale[r : r + chunk]
+                rows = rows.astype(jnp.bfloat16).astype(jnp.float32)
+                for j in range(groups):
+                    first = (o * stations + r) * groups + j
+                    panel[pl.ds(first, chunk, stride=groups), :] = rows[:, j * 128 : j * 128 + 128]
+            return carry
+
+        lax.fori_loop(0, owners, whiten, 0)
+
+    pairs = ids_ref.shape[0] // 2
+
+    def fetch(i, carry):
+        for u in range(16):
+            p = i * 16 + u
+            here = pl.ds(pl.multiple_of(p * groups, groups), groups)
+            a = pl.multiple_of(ids_ref[step * tile + p], groups)
+            b = pl.multiple_of(ids_ref[pairs + step * tile + p], groups)
+            near[here, :] = panel[pl.ds(a, groups), :]
+            far[here, :] = panel[pl.ds(b, groups), :]
+        return carry
+
+    lax.fori_loop(0, tile // 16, fetch, 0)
+
+    def multiply(i, carry):
+        rows = pl.ds(pl.multiple_of(i * chunk, chunk), chunk)
+        for j in range(fold):
+            re = pl.ds(i * chunk * groups + j, chunk, stride=groups)
+            im = pl.ds(i * chunk * groups + j + fold, chunk, stride=groups)
+            ar, ai, br, bi = near[re, :], near[im, :], far[re, :], far[im, :]
+            cross[rows, j * 128 : j * 128 + 128] = (ar * br + ai * bi).astype(jnp.bfloat16)
+            cross[rows, half + j * 128 : half + j * 128 + 128] = (ai * br - ar * bi).astype(
+                jnp.bfloat16
+            )
+        return carry
+
+    lax.fori_loop(0, tile // chunk, multiply, 0)
+
+    lagged = jnp.dot(cross[...], table_ref[...], preferred_element_type=jnp.float32)
+    lag = lax.broadcasted_iota(jnp.int32, lagged.shape, 1)
+    inside = (lag >= window_ref[:, 0:1]) & (lag < window_ref[:, 1:2])
+    residual = jnp.where(inside, lagged - observed_ref[...].astype(jnp.float32), 0.0)
+    adjoint = jnp.dot(
+        residual.astype(jnp.bfloat16), back_ref[...], preferred_element_type=jnp.float32
+    )
+    spec = cross[...].astype(jnp.float32)
+    out_ref[...] = (
+        adjoint[:, :half] * spec[:, :half] + adjoint[:, half:] * spec[:, half:]
+    ).astype(jnp.bfloat16)
+
+
+def sum_kernel(
+    ids_ref, kernel_ref, out_ref,
+    sums, side_send, side_recv, diag_send, diag_across, diag_along, far_send, far_recv,
+    side_ss, side_rs, send_sem, recv_sem,
+):
+    me = lax.axis_index("pairs")
+    across, along, diagonal, sibling = neighbours(me)
+    stations, width = out_ref.shape
+    half = stations // 2
+    shift = 1 - 2 * (me % 2)
+
+    barrier = pltpu.get_barrier_semaphore()
+    for peer in (across, along, sibling):
+        pl.semaphore_signal(barrier, inc=1, device_id={"pairs": peer}, device_id_type=MESH)
+    pl.semaphore_wait(barrier, 3)
+
+    def partial(owner, first):
+        here = lax.broadcasted_iota(jnp.int32, (half, ids_ref.shape[1]), 0)
+        base = owner * stations + first
+        hit = (here == ids_ref[0:1, :] - base) | (here == ids_ref[1:2, :] - base)
+        return jnp.dot(
+            hit.astype(jnp.bfloat16), kernel_ref[...], preferred_element_type=jnp.float32
+        )
+
+    def send(src, dst, sem, target):
+        copy = pltpu.make_async_remote_copy(
+            src_ref=src, dst_ref=dst, send_sem=send_sem.at[sem], recv_sem=recv_sem.at[sem],
+            device_id={"pairs": target}, device_id_type=MESH,
+        )
+        copy.start()
+        return copy
+
+    low, high = pl.ds(0, half), pl.ds(half, half)
+    sides = []
+
+    def chip_sum(q, chip):
+        def other(i, carry):
+            first = pl.multiple_of(i * half, half)
+            side_send[q, pl.ds(first, half), :] = partial(chip + shift, first).astype(
+                jnp.bfloat16
+            )
+            return carry
+
+        lax.fori_loop(0, 2, other, 0)
+        copy = pltpu.make_async_remote_copy(
+            src_ref=side_send.at[q], dst_ref=side_recv.at[q], send_sem=side_ss.at[q],
+            recv_sem=side_rs.at[q], device_id={"pairs": sibling}, device_id_type=MESH,
+        )
+        copy.start()
+        sides.append(copy)
+
+        def mine(i, carry):
+            first = pl.multiple_of(i * half, half)
+            sums[q, pl.ds(first, half), :] = partial(chip, first)
+            return carry
+
+        lax.fori_loop(0, 2, mine, 0)
+        copy.wait_recv()
+
+    def whole(q, rows):
+        return sums[q, rows, :] + side_recv[q, rows, :].astype(jnp.float32)
+
+    chip_sum(0, diagonal)
+    diag_send[low, :] = whole(0, low).astype(jnp.bfloat16)
+    to_across = send(diag_send.at[low], diag_across, 0, across)
+    diag_send[high, :] = whole(0, high).astype(jnp.bfloat16)
+    to_along = send(diag_send.at[high], diag_along, 1, along)
+
+    chip_sum(1, across)
+    far_send[0, low, :] = whole(1, low).astype(jnp.bfloat16)
+    first_across = send(far_send.at[0, low], far_recv.at[0, low], 2, across)
+    chip_sum(2, along)
+    far_send[1, high, :] = whole(2, high).astype(jnp.bfloat16)
+    first_along = send(far_send.at[1, high], far_recv.at[1, high], 3, along)
+
+    to_along.wait_recv()
+    far_send[0, high, :] = (whole(1, high) + diag_along[...].astype(jnp.float32)).astype(
+        jnp.bfloat16
+    )
+    last_across = send(far_send.at[0, high], far_recv.at[0, high], 4, across)
+    to_across.wait_recv()
+    far_send[1, low, :] = (whole(2, low) + diag_across[...].astype(jnp.float32)).astype(
+        jnp.bfloat16
+    )
+    last_along = send(far_send.at[1, low], far_recv.at[1, low], 5, along)
+
+    chip_sum(3, me)
+    for copy in (first_across, first_along, last_across, last_along):
+        copy.wait_recv()
+    for rows in (low, high):
+        out_ref[rows, :] = 0.25 * (
+            whole(3, rows)
+            + far_recv[0, rows, :].astype(jnp.float32)
+            + far_recv[1, rows, :].astype(jnp.float32)
+        )
+    for copy in (to_across, to_along, first_across, first_along, last_across, last_along):
+        copy.wait_send()
+    for copy in sides:
+        copy.wait_send()
+
+
+def chip_shards(spectra, observed, pair_owner, pair_slot, win_start, win_end):
+    owners = lax.axis_size("pairs")
+    bands = lax.axis_size("band")
+    stations, _, width = spectra.shape
+    half = width // 2
+    pairs, _, lags = observed.shape
+    tile = min(256, pairs)
+    bf16, f32 = jnp.bfloat16, jnp.float32
+    vmem = pl.BlockSpec(memory_space=pltpu.VMEM)
+    hbm = pl.BlockSpec(memory_space=pl.ANY)
+    dma = pltpu.SemaphoreType.DMA
+
+    spectra = spectra.reshape(stations, width)
+    observed = observed.reshape(pairs, lags)
+    ids = (pair_owner * stations + pair_slot).astype(jnp.int32).T
+    window = jnp.stack([win_start, win_end], axis=1)
+    table = basis_constant(half, lags)
+
+    with jax.named_scope("spread_spectra"):
+        panel, scale = pl.pallas_call(
+            functools.partial(gather_kernel, bands, bands * width, owners),
+            out_shape=(
+                jax.ShapeDtypeStruct((owners, stations, width), bf16),
+                jax.ShapeDtypeStruct((owners, 8, stations), f32),
+            ),
+            in_specs=[vmem, hbm],
+            out_specs=(hbm, vmem),
+            scratch_shapes=[
+                pltpu.VMEM((8, stations), f32),
+                pltpu.VMEM((bands, 8, stations), f32),
+                pltpu.VMEM((8, stations), f32),
+                pltpu.VMEM((owners, 8, stations), f32),
+                dma, dma((14,)), dma((14,)), dma((bands,)), dma((bands,)),
+                dma((owners,)), dma((owners,)),
+            ],
+            compiler_params=pltpu.CompilerParams(
+                collective_id=0, has_side_effects=True, vmem_limit_bytes=VMEM_LIMIT
+            ),
+        )(spectra, spectra)
+
+    once = pl.Buffered(1)
+    with jax.named_scope("pair_kernels"):
+        kernels = pl.pallas_call(
+            pair_kernel,
+            out_shape=jax.ShapeDtypeStruct((pairs, half), bf16),
+            grid_spec=pltpu.PrefetchScalarGridSpec(
+                num_scalar_prefetch=1,
+                grid=(pairs // tile,),
+                in_specs=[
+                    pl.BlockSpec(
+                        (owners, stations, width), lambda i, s: (0, 0, 0), pipeline_mode=once
+                    ),
+                    pl.BlockSpec(
+                        (owners, 8, stations), lambda i, s: (0, 0, 0), pipeline_mode=once
+                    ),
+                    pl.BlockSpec((tile, lags), lambda i, s: (i, 0)),
+                    pl.BlockSpec((tile, 2), lambda i, s: (i, 0)),
+                    pl.BlockSpec((width, lags), lambda i, s: (0, 0), pipeline_mode=once),
+                    pl.BlockSpec((lags, width), lambda i, s: (0, 0), pipeline_mode=once),
+                ],
+                out_specs=pl.BlockSpec((tile, half), lambda i, s: (i, 0)),
+                scratch_shapes=[
+                    pltpu.VMEM((owners * stations * width // 128, 128), f32),
+                    pltpu.VMEM((tile * width // 128, 128), f32),
+                    pltpu.VMEM((tile * width // 128, 128), f32),
+                    pltpu.VMEM((tile, width), bf16),
+                ],
+            ),
+            compiler_params=pltpu.CompilerParams(vmem_limit_bytes=VMEM_LIMIT),
+        )(
+            (ids * (width // 128)).reshape(-1),
+            panel,
+            scale,
+            observed,
+            window,
+            jnp.asarray(table, bf16),
+            jnp.asarray(table.T, bf16),
+        )
+
+    with jax.named_scope("station_sums"):
+        out = pl.pallas_call(
+            sum_kernel,
+            out_shape=jax.ShapeDtypeStruct((stations, half), f32),
+            in_specs=[vmem, vmem],
+            out_specs=vmem,
+            scratch_shapes=[
+                pltpu.VMEM((4, stations, half), f32),
+                pltpu.VMEM((4, stations, half), bf16),
+                pltpu.VMEM((4, stations, half), bf16),
+                pltpu.VMEM((stations, half), bf16),
+                pltpu.VMEM((stations // 2, half), bf16),
+                pltpu.VMEM((stations // 2, half), bf16),
+                pltpu.VMEM((2, stations, half), bf16),
+                pltpu.VMEM((2, stations, half), bf16),
+                dma((4,)), dma((4,)), dma((6,)), dma((6,)),
+            ],
+            compiler_params=pltpu.CompilerParams(
+                collective_id=1, has_side_effects=True, vmem_limit_bytes=VMEM_LIMIT
+            ),
+        )(ids, kernels)
+    return out.reshape(stations, 1, half)
 
 
 def lag_basis(half_width, lag_count):
@@ -105,8 +513,9 @@
 
 
 def solution(mesh):
+    square_of_chips = mesh.shape["pairs"] == 8
     return jax.shard_map(
-        shards,
+        chip_shards if square_of_chips else shards,
         mesh=mesh,
         in_specs=(
             P("pairs", "band", None),

time: 529 us -> 111 us (0.21); the launches traced: 521 us -> 110 us
  local copies, waits for them, and re-layouts: 180 us -> 5.22 us
  waiting for transfers between devices: 156 us -> 0 us
  other arithmetic: 131 us -> 2.08 us
  Pallas kernels: 0 us -> 103 us
  matrix products: 16.3 us -> 0 us
  between operations: 13.9 us -> 0.02 us
  blocking collectives: 13.5 us -> 0 us
  starting transfers between devices: 9.87 us -> 0 us
    all_to_all x2 -> x0, waiting for transfers between devices: 139 us -> none  [the longest x1 139 us: shards(): lax.all_to_all(outgoing, 'pairs', split_axis=0, concat_axis=0, tiled=True)]
    pallas_call x0 -> x3, Pallas kernels: none -> 103 us  [the longest x1 47.4 us: chip_shards(): pl.pallas_call(functools.partial(gather_kernel, bands, bands * width, own...]
    unnamed x23 -> x1, local copies, waits for them, and re-layouts: 84.7 us -> 0.6 us
    scatter-add x8 -> x0, other arithmetic: 83.9 us -> none  [add_source(): return summed.at[block_ids].add(block_rows)]
    gather x1 -> x0, local copies, waits for them, and re-layouts: 25.4 us -> none  [shards(): fetched = panel_rows[owner_flat * station_count + slot_flat]]
    reshape x5 -> x1, local copies, waits for them, and re-layouts: 28.2 us -> 3.27 us  [chip_shards(): return out.reshape(stations, 1, half)]
    another operation x1, local copies, waits for them, and re-layouts: 21.4 us -> 1.35 us  [chip_shards(): window = jnp.stack([win_start, win_end], axis=1)]
    slice x2 -> x0, local copies, waits for them, and re-layouts: 17.5 us -> none  [the longest x1 17.2 us: shards(): far_end = fetched[:, 1].astype(jnp.float32)]
  transfers between devices with their start and end apart: 3 -> 0, of which waited for: 2 -> 0; matrix products, arithmetic and copies ran while one was open for 45% -> 0% of each run, Pallas kernels for 0% -> 0%
where the time goes in v1:
time: 111 us; the launch traced here: 110 us
  Pallas kernels  103 us (93%)
  local copies, waits for them, and re-layouts  5.22 us (5%)
  other arithmetic  2.08 us (2%)
    pallas_call x1, Pallas kernels, chip_shards(): pl.pallas_call(functools.partial(gather_kernel, bands, bands * width, own...  47.4 us
    pallas_call x1, Pallas kernels, chip_shards(): pl.pallas_call(pair_kernel, out_shape=jax.ShapeDtypeStruct((pairs, half),...  28.9 us
    pallas_call x1, Pallas kernels, chip_shards(): pl.pallas_call(sum_kernel, out_shape=jax.ShapeDtypeStruct((stations, half...  26.8 us
    reshape x1, local copies, waits for them, and re-layouts, chip_shards(): return out.reshape(stations, 1, half)  3.27 us

profile of v1, /device:TPU:0, one launch (start us, length us, event | category | flops | bytes accessed | tf_op | source)
XLA Modules:
  0.0 110.5 jit_solution(1743997540179432136)
XLA Ops:
  0.0 0.7 pad_add_fusion
  0.7 1.4 %multiply_bitcast_fusion = (s32[1,16,2,128]{3,2,1,0:T(2,128)S(1)}, s32[2,2048]{1,0:T(2,128)}) fusion(s32[2048,2]{0,1:T(2,128)} %param.11, s32[2048,2]{0,1:T(2,128)} %param.10), kind=kLoop, calls=%fused_computation.1 | loop fusion | flops 12288 | bytes 65536
  2.1 0.6 copy.15
  2.7 1.3 %copy.13.window_ref = s32[2048,2]{1,0:T(8,128)} copy(s32[2048,2]{0,1:T(2,128)S(1)} %pad_add_fusion) | data formatting | bytes 32768 | tf_op jit(solution)/shard_map/stack | solution.py:329
  4.0 47.4 %spread_spectra.1 = (bf16[8,512,1024]{2,1,0:T(8,128)(2,1)}, f32[8,8,512]{2,1,0:T(8,128)}) custom-call(bf16[512,1024]{1,0:T(8,128)(2,1)} %bitcast.12, bf16[512,1024]{1,0:T(8,128)(2,1)} %bitcast.13), custom_call_target="tpu_custom_call" | custom-call | tf_op jit(solution)/shard_map/spread_spectra/pallas_call | solution.py:333
  51.4 28.9 %pair_kernels.1.kernel_ref = bf16[2048,512]{1,0:T(8,128)(2,1)} custom-call(s32[4096]{0:T(1024)} %bitcast.15, bf16[8,512,1024]{2,1,0:T(8,128)(2,1)} %get-tuple-element.7.arr_ref, f32[8,8,512]{2,1,0:T(8,128)} %get-tuple-element.8.scale_ref, bf16[2048,1024]{1,0:T(8,128)(2,1)} %bitcast.14, s32[2048,2]{1,0:T(8,128)} %copy.13.window_ref, ...), custom_call_target="tpu_custom_call" | custom-call | tf_op jit(solution)/shard_map/pair_kernels/pallas_call | solution.py:356
  80.3 26.8 %station_sums.1 = f32[512,512]{1,0:T(8,128)} custom-call(s32[2,2048]{1,0:T(2,128)} %get-tuple-element.10.ids_ref, bf16[2048,512]{1,0:T(8,128)(2,1)} %pair_kernels.1.kernel_ref), custom_call_target="tpu_custom_call" | custom-call | tf_op jit(solution)/shard_map/station_sums/pallas_call | solution.py:394
  107.2 3.3 %copy.14 = f32[512,1,512]{2,1,0:T(1,128)} copy(f32[512,1,512]{2,0,1:T(8,128)} %bitcast.11) | data formatting | bytes 2097152 | tf_op jit(solution)/shard_map/reshape | solution.py:414

commit v2 on v0

--- a/solution.py
+++ b/solution.py
@@ -1,9 +1,437 @@
+import functools
 import math
 
 import jax
 import jax.numpy as jnp
+import numpy as np
 from jax import lax
+from jax.experimental import pallas as pl
+from jax.experimental.pallas import tpu as pltpu
 from jax.sharding import PartitionSpec as P
+
+MESH = pl.DeviceIdType.MESH
+VMEM_LIMIT = 60 * 1024 * 1024
+
+
+def basis_constant(half_width, lag_count):
+    phases = (np.arange(half_width)[:, None] * np.arange(lag_count)[None, :] % lag_count) * (
+        2.0 * math.pi / lag_count
+    )
+    factor = 1.0 / math.sqrt(lag_count)
+    table = np.concatenate([np.cos(phases) * factor, -np.sin(phases) * factor], axis=0)
+    return table.astype(np.float32)
+
+
+def neighbours(me):
+    core, x, y = me % 2, (me // 2) % 2, me // 4
+    across, along = me + 2 - 4 * x, me + 4 - 8 * y
+    return across, along, across + 4 - 8 * y, me + 1 - 2 * core
+
+
+def pair_kernel(
+    bands, owners, tile,
+    spec_ref, ids_ref, start_ref, end_ref, observed_hbm, table_hbm, back_hbm, out_ref,
+    arr, panel, near, far, cross, lagged, observed, table, back, edges,
+    part, part_recv, total, total_recv,
+    local_sem, send_sem, recv_sem, band_send, band_recv, total_send, total_recv_sem,
+):
+    me = lax.axis_index("pairs")
+    band = lax.axis_index("band")
+    across, along, diagonal, sibling = neighbours(me)
+    shift = 1 - 2 * (me % 2)
+    stations, width = spec_ref.shape
+    pairs, lags = observed.shape
+    piece = width // 2
+    bins = piece // 2
+    groups = width // 128
+    fold = groups // 4
+    half = stations // 2
+    chunk = 64
+    names = {}
+    panel_rows = panel.reshape(owners * stations * groups, 128)
+
+    barrier = pltpu.get_barrier_semaphore()
+    for k in range(1, owners):
+        pl.semaphore_signal(
+            barrier, inc=1, device_id={"pairs": lax.rem(me + k, owners)}, device_id_type=MESH
+        )
+    for k in range(1, bands):
+        pl.semaphore_signal(
+            barrier, inc=1, device_id={"band": lax.rem(band + k, bands)}, device_id_type=MESH
+        )
+    loads = []
+    for source, target in ((table_hbm, table), (back_hbm, back), (observed_hbm, observed)):
+        loads.append(pltpu.make_async_copy(source, target, local_sem.at[len(loads)]))
+        loads[-1].start()
+    for h in range(2):
+        arr[h, me, :, 0:bins] = spec_ref[:, h * bins : h * bins + bins]
+        arr[h, me, :, bins:piece] = spec_ref[:, piece + h * bins : piece + h * bins + bins]
+    pl.semaphore_wait(barrier, owners + bands - 2)
+
+    sent = []
+
+    def transfer(h, owner, rows, key, target):
+        place = arr.at[h, owner] if rows is None else arr.at[h, owner, pl.ds(rows * half, half)]
+        sem = names.setdefault((key, h, rows), len(names))
+        return pltpu.make_async_remote_copy(
+            src_ref=place, dst_ref=place, send_sem=send_sem.at[sem], recv_sem=recv_sem.at[sem],
+            device_id={"pairs": target}, device_id_type=MESH,
+        )
+
+    def push(*message):
+        sent.append(transfer(*message))
+        sent[-1].start()
+
+    def arrived(h, owner, rows, key):
+        transfer(h, owner, rows, key, sibling).wait_recv()
+
+    def push_own(h):
+        push(h, me, 0, "x", across)
+        push(h, me, 1, "y", along)
+        push(h, me, 1, "x", across)
+        push(h, me, 0, "y", along)
+        push(h, me, None, "own", sibling)
+
+    def forward(h):
+        arrived(h, across, 0, "x")
+        push(h, across, 0, "diagonal", along)
+        arrived(h, along, 1, "y")
+        push(h, along, 1, "diagonal", across)
+
+    def whiten(h, o):
+        scale = total_recv[o].T[:, 0:1]
+        for r in range(0, stations, chunk):
+            rows = arr[h, o, r : r + chunk, :].astype(jnp.float32) * scale[r : r + chunk]
+            rows = rows.astype(jnp.bfloat16).astype(jnp.float32)
+            for j in range(groups // 2):
+                first = (o * stations + r) * groups + h * (groups // 2) + j
+                panel_rows[pl.ds(first, chunk, stride=groups), :] = rows[
+                    :, j * 128 : j * 128 + 128
+                ]
+
+    def share(h):
+        arrived(h, across, 1, "x")
+        push(h, across, None, "over x", sibling)
+        arrived(h, along, 0, "y")
+        push(h, along, None, "over y", sibling)
+        whiten(h, across)
+        whiten(h, along)
+        arrived(h, me + shift, None, "own")
+        whiten(h, me + shift)
+
+    def finish(h):
+        arrived(h, diagonal, 0, "diagonal")
+        arrived(h, diagonal, 1, "diagonal")
+        push(h, diagonal, None, "over both", sibling)
+        arrived(h, across + shift, None, "over x")
+        whiten(h, across + shift)
+        arrived(h, along + shift, None, "over y")
+        whiten(h, along + shift)
+        whiten(h, diagonal)
+        arrived(h, diagonal + shift, None, "over both")
+        whiten(h, diagonal + shift)
+
+    push_own(0)
+
+    spectrum = spec_ref[...].astype(jnp.float32)
+    square = spectrum * spectrum
+    upper = square.astype(jnp.bfloat16)
+    lower = (square - upper.astype(jnp.float32)).astype(jnp.bfloat16)
+    ones = jnp.ones((8, width), jnp.bfloat16)
+    dims = (((1,), (1,)), ((), ()))
+    part[...] = lax.dot_general(
+        ones, upper, dims, preferred_element_type=jnp.float32
+    ) + lax.dot_general(ones, lower, dims, preferred_element_type=jnp.float32)
+    copies = []
+    for k in range(1, bands):
+        copies.append(
+            pltpu.make_async_remote_copy(
+                src_ref=part, dst_ref=part_recv.at[k], send_sem=band_send.at[k],
+                recv_sem=band_recv.at[k],
+                device_id={"band": lax.rem(band + k, bands)}, device_id_type=MESH,
+            )
+        )
+        copies[-1].start()
+    for copy in copies:
+        copy.wait()
+    power = part[...]
+    for k in range(1, bands):
+        power = power + part_recv[k]
+    total[...] = lax.rsqrt(power / (bands * width) + 1e-05)
+    total_recv[me] = total[...]
+    copies = []
+    for k in range(1, owners):
+        copies.append(
+            pltpu.make_async_remote_copy(
+                src_ref=total, dst_ref=total_recv.at[me], send_sem=total_send.at[k],
+                recv_sem=total_recv_sem.at[k],
+                device_id={"pairs": lax.rem(me + k, owners)}, device_id_type=MESH,
+            )
+        )
+        copies[-1].start()
+    for t in range(0, pairs, tile):
+        for side, source in enumerate((start_ref, end_ref)):
+            column = jnp.broadcast_to(source[0:1, t : t + tile], (8, tile)).T
+            edges[t : t + tile, side : side + 1] = column[:, 0:1]
+    whiten(0, me)
+    for copy in copies:
+        copy.wait()
+
+    def fetch_tile(h, t):
+        def fetch(i, carry):
+            for u in range(16):
+                p = i * 16 + u
+                here = pl.ds(pl.multiple_of(p * groups, groups), groups)
+                near[here, :] = panel[ids_ref[0, t * tile + p]]
+                far[here, :] = panel[ids_ref[1, t * tile + p]]
+            return carry
+
+        lax.fori_loop(0, tile // 16, fetch, 0)
+
+        def multiply(i, carry):
+            rows = pl.ds(pl.multiple_of(t * tile + i * chunk, chunk), chunk)
+            for j in range(fold):
+                first = i * chunk * groups + h * (groups // 2) + j
+                re = pl.ds(first, chunk, stride=groups)
+                im = pl.ds(first + fold, chunk, stride=groups)
+                ar, ai, br, bi = near[re, :], near[im, :], far[re, :], far[im, :]
+                cross[h, rows, j * 128 : j * 128 + 128] = (ar * br + ai * bi).astype(jnp.bfloat16)
+                cross[h, rows, bins + j * 128 : bins + j * 128 + 128] = (
+                    ai * br - ar * bi
+                ).astype(jnp.bfloat16)
+            return carry
+
+        lax.fori_loop(0, tile // chunk, multiply, 0)
+
+    def first_piece(t, carry):
+        rows = pl.ds(pl.multiple_of(t * tile, tile), tile)
+        fetch_tile(0, t)
+        lagged[rows, :] = jnp.dot(
+            cross[0, rows, :], table[0:piece, :], preferred_element_type=jnp.float32
+        )
+        return carry
+
+    def second_piece(t, carry):
+        rows = pl.ds(pl.multiple_of(t * tile, tile), tile)
+        fetch_tile(1, t)
+        sums = lagged[rows, :] + jnp.dot(
+            cross[1, rows, :], table[piece:width, :], preferred_element_type=jnp.float32
+        )
+        lag = lax.broadcasted_iota(jnp.int32, sums.shape, 1)
+        inside = (lag >= edges[rows, 0:1]) & (lag < edges[rows, 1:2])
+        residual = jnp.where(inside, sums - observed[rows, :].astype(jnp.float32), 0.0)
+        residual = residual.astype(jnp.bfloat16)
+        for h in range(2):
+            adjoint = jnp.dot(
+                residual,
+                back[:, h * piece : h * piece + piece],
+                preferred_element_type=jnp.float32,
+            )
+            spec = cross[h, rows, :].astype(jnp.float32)
+            out_ref[rows, h * bins : h * bins + bins] = (
+                adjoint[:, :bins] * spec[:, :bins] + adjoint[:, bins:] * spec[:, bins:]
+            ).astype(jnp.bfloat16)
+        return carry
+
+    tiles = pairs // tile
+    forward(0)
+    push_own(1)
+    share(0)
+    finish(0)
+    for copy in loads:
+        copy.wait()
+    lax.fori_loop(0, tiles // 2, first_piece, 0)
+    forward(1)
+    lax.fori_loop(tiles // 2, tiles, first_piece, 0)
+    whiten(1, me)
+    share(1)
+    finish(1)
+    lax.fori_loop(0, tiles, second_piece, 0)
+    for copy in sent:
+        copy.wait_send()
+
+
+def sum_kernel(
+    stations, owner_ref, slot_ref, kernel_ref, out_ref,
+    sums, side_send, side_recv, diag_send, diag_across, diag_along, far_send, far_recv,
+    side_ss, side_rs, send_sem, recv_sem,
+):
+    me = lax.axis_index("pairs")
+    across, along, diagonal, sibling = neighbours(me)
+    groups = kernel_ref.shape[1] // 128
+    half = stations // 2
+    shift = 1 - 2 * (me % 2)
+
+    barrier = pltpu.get_barrier_semaphore()
+    for peer in (across, along, sibling):
+        pl.semaphore_signal(barrier, inc=1, device_id={"pairs": peer}, device_id_type=MESH)
+    pl.semaphore_wait(barrier, 3)
+
+    def partial(owner, first):
+        here = lax.broadcasted_iota(jnp.int32, (half, slot_ref.shape[1]), 0)
+        place = jnp.where(owner_ref[...] == owner, slot_ref[...] - first, -1)
+        hit = (here == place[0:1, :]) | (here == place[1:2, :])
+        return jnp.dot(
+            hit.astype(jnp.bfloat16), kernel_ref[...], preferred_element_type=jnp.float32
+        )
+
+    def send(src, dst, sem, target):
+        copy = pltpu.make_async_remote_copy(
+            src_ref=src, dst_ref=dst, send_sem=send_sem.at[sem], recv_sem=recv_sem.at[sem],
+            device_id={"pairs": target}, device_id_type=MESH,
+        )
+        copy.start()
+        return copy
+
+    low, high = pl.ds(0, half), pl.ds(half, half)
+    sides = []
+
+    def chip_sum(q, chip):
+        def other(i, carry):
+            first = pl.multiple_of(i * half, half)
+            side_send[q, pl.ds(first, half), :] = partial(chip + shift, first).astype(
+                jnp.bfloat16
+            )
+            return carry
+
+        lax.fori_loop(0, 2, other, 0)
+        copy = pltpu.make_async_remote_copy(
+            src_ref=side_send.at[q], dst_ref=side_recv.at[q], send_sem=side_ss.at[q],
+            recv_sem=side_rs.at[q], device_id={"pairs": sibling}, device_id_type=MESH,
+        )
+        copy.start()
+        sides.append(copy)
+
+        def mine(i, carry):
+            first = pl.multiple_of(i * half, half)
+            sums[q, pl.ds(first, half), :] = partial(chip, first)
+            return carry
+
+        lax.fori_loop(0, 2, mine, 0)
+        copy.wait_recv()
+
+    def whole(q, rows):
+        return sums[q, rows, :] + side_recv[q, rows, :].astype(jnp.float32)
+
+    chip_sum(0, diagonal)
+    diag_send[low, :] = whole(0, low).astype(jnp.bfloat16)
+    to_across = send(diag_send.at[low], diag_across, 0, across)
+    diag_send[high, :] = whole(0, high).astype(jnp.bfloat16)
+    to_along = send(diag_send.at[high], diag_along, 1, along)
+
+    chip_sum(1, across)
+    far_send[0, low, :] = whole(1, low).astype(jnp.bfloat16)
+    first_across = send(far_send.at[0, low], far_recv.at[0, low], 2, across)
+    chip_sum(2, along)
+    far_send[1, high, :] = whole(2, high).astype(jnp.bfloat16)
+    first_along = send(far_send.at[1, high], far_recv.at[1, high], 3, along)
+
+    to_along.wait_recv()
+    far_send[0, high, :] = (whole(1, high) + diag_along[...].astype(jnp.float32)).astype(
+        jnp.bfloat16
+    )
+    last_across = send(far_send.at[0, high], far_recv.at[0, high], 4, across)
+    to_across.wait_recv()
+    far_send[1, low, :] = (whole(2, low) + diag_across[...].astype(jnp.float32)).astype(
+        jnp.bfloat16
+    )
+    last_along = send(far_send.at[1, low], far_recv.at[1, low], 5, along)
+
+    chip_sum(3, me)
+    for copy in (first_across, first_along, last_across, last_along):
+        copy.wait_recv()
+    for first in (0, half):
+        rows = pl.ds(first, half)
+        result = 0.25 * (
+            whole(3, rows)
+            + far_recv[0, rows, :].astype(jnp.float32)
+            + far_recv[1, rows, :].astype(jnp.float32)
+        )
+        for j in range(groups):
+            out_ref[pl.ds(first * groups + j, half, stride=groups), :] = result[
+                :, j * 128 : j * 128 + 128
+            ]
+    for copy in (to_across, to_along, first_across, first_along, last_across, last_along):
+        copy.wait_send()
+    for copy in sides:
+        copy.wait_send()
+
+
+def chip_shards(spectra, observed, pair_owner, pair_slot, win_start, win_end):
+    owners = lax.axis_size("pairs")
+    bands = lax.axis_size("band")
+    stations, _, width = spectra.shape
+    half = width // 2
+    pairs, _, lags = observed.shape
+    tile = min(256, pairs)
+    bf16, f32 = jnp.bfloat16, jnp.float32
+    vmem = pl.BlockSpec(memory_space=pltpu.VMEM)
+    hbm = pl.BlockSpec(memory_space=pl.ANY)
+    dma = pltpu.SemaphoreType.DMA
+
+    table = basis_constant(half, lags).reshape(2, 2, half // 2, lags)
+    table = table.transpose(1, 0, 2, 3).reshape(width, lags)
+    owner_rows, slot_rows = pair_owner.T, pair_slot.T
+
+    with jax.named_scope("pair_kernels"):
+        kernels = pl.pallas_call(
+            functools.partial(pair_kernel, bands, owners, tile),
+            out_shape=jax.ShapeDtypeStruct((pairs, half), bf16),
+            in_specs=[vmem, pl.BlockSpec(memory_space=pltpu.SMEM), vmem, vmem] + [hbm] * 3,
+            out_specs=vmem,
+            scratch_shapes=[
+                pltpu.VMEM((2, owners, stations, half), bf16),
+                pltpu.VMEM((owners * stations, width // 128, 128), f32),
+                pltpu.VMEM((tile * width // 128, 128), f32),
+                pltpu.VMEM((tile * width // 128, 128), f32),
+                pltpu.VMEM((2, pairs, half), bf16),
+                pltpu.VMEM((pairs, lags), f32),
+                pltpu.VMEM((pairs, lags), bf16),
+                pltpu.VMEM((width, lags), bf16),
+                pltpu.VMEM((lags, width), bf16),
+                pltpu.VMEM((pairs, 2), jnp.int32),
+                pltpu.VMEM((8, stations), f32),
+                pltpu.VMEM((bands, 8, stations), f32),
+                pltpu.VMEM((8, stations), f32),
+                pltpu.VMEM((owners, 8, stations), f32),
+                dma((3,)), dma((20,)), dma((20,)), dma((bands,)), dma((bands,)),
+                dma((owners,)), dma((owners,)),
+            ],
+            compiler_params=pltpu.CompilerParams(
+                collective_id=0, has_side_effects=True, vmem_limit_bytes=VMEM_LIMIT
+            ),
+        )(
+            spectra.reshape(stations, width),
+            owner_rows * stations + slot_rows,
+            win_start.reshape(1, pairs),
+            win_end.reshape(1, pairs),
+            observed.reshape(pairs, lags),
+            jnp.asarray(table, bf16),
+            jnp.asarray(table.T, bf16),
+        )
+
+    with jax.named_scope("station_sums"):
+        out = pl.pallas_call(
+            functools.partial(sum_kernel, stations),
+            out_shape=jax.ShapeDtypeStruct((stations * half // 128, 128), f32),
+            in_specs=[vmem] * 3,
+            out_specs=vmem,
+            scratch_shapes=[
+                pltpu.VMEM((4, stations, half), f32),
+                pltpu.VMEM((4, stations, half), bf16),
+                pltpu.VMEM((4, stations, half), bf16),
+                pltpu.VMEM((stations, half), bf16),
+                pltpu.VMEM((stations // 2, half), bf16),
+                pltpu.VMEM((stations // 2, half), bf16),
+                pltpu.VMEM((2, stations, half), bf16),
+                pltpu.VMEM((2, stations, half), bf16),
+                dma((4,)), dma((4,)), dma((6,)), dma((6,)),
+            ],
+            compiler_params=pltpu.CompilerParams(
+                collective_id=1, has_side_effects=True, vmem_limit_bytes=VMEM_LIMIT
+            ),
+        )(owner_rows, slot_rows, kernels)
+    return out.reshape(stations, 1, half)
 
 
 def lag_basis(half_width, lag_count):
@@ -105,8 +533,9 @@
 
 
 def solution(mesh):
+    square_of_chips = mesh.shape["pairs"] == 8
     return jax.shard_map(
-        shards,
+        chip_shards if square_of_chips else shards,
         mesh=mesh,
         in_specs=(
             P("pairs", "band", None),

time: 529 us -> 101 us (0.19); the launches traced: 521 us -> 100 us
  local copies, waits for them, and re-layouts: 180 us -> 2.91 us
  waiting for transfers between devices: 156 us -> 0 us
  other arithmetic: 131 us -> 1.35 us
  Pallas kernels: 0 us -> 95.9 us
  matrix products: 16.3 us -> 0 us
  between operations: 13.9 us -> 0.02 us
  blocking collectives: 13.5 us -> 0 us
  starting transfers between devices: 9.87 us -> 0 us
    all_to_all x2 -> x0, waiting for transfers between devices: 139 us -> none  [the longest x1 139 us: shards(): lax.all_to_all(outgoing, 'pairs', split_axis=0, concat_axis=0, tiled=True)]
    pallas_call x0 -> x2, Pallas kernels: none -> 95.9 us  [the longest x1 69.1 us: chip_shards(): pl.pallas_call(functools.partial(pair_kernel, bands, owners, tile), out_s...]
    scatter-add x8 -> x0, other arithmetic: 83.9 us -> none  [add_source(): return summed.at[block_ids].add(block_rows)]
    unnamed x23 -> x1, local copies, waits for them, and re-layouts: 84.7 us -> 2.91 us
    reshape x5 -> x0, local copies, waits for them, and re-layouts: 28.2 us -> none  [the longest x1 13.3 us: shards(): jnp.stack([to_first, to_second], axis=1)]
    gather x1 -> x0, local copies, waits for them, and re-layouts: 25.4 us -> none  [shards(): fetched = panel_rows[owner_flat * station_count + slot_flat]]
    another operation x1 -> x0, local copies, waits for them, and re-layouts: 21.4 us -> none  [shards(): jnp.stack([to_first, to_second], axis=1)]
    slice x2 -> x0, local copies, waits for them, and re-layouts: 17.5 us -> none  [the longest x1 17.2 us: shards(): far_end = fetched[:, 1].astype(jnp.float32)]
  transfers between devices with their start and end apart: 3 -> 0, of which waited for: 2 -> 0; matrix products, arithmetic and copies ran while one was open for 45% -> 0% of each run, Pallas kernels for 0% -> 0%
where the time goes in v2:
time: 101 us; the launch traced here: 100 us
  Pallas kernels  95.9 us (95%)
  local copies, waits for them, and re-layouts  2.91 us (3%)
  other arithmetic  1.35 us (1%)
    pallas_call x1, Pallas kernels, chip_shards(): pl.pallas_call(functools.partial(pair_kernel, bands, owners, tile), out_s...  69.1 us
    pallas_call x1, Pallas kernels, chip_shards(): pl.pallas_call(functools.partial(sum_kernel, stations), out_shape=jax.Sha...  26.9 us
    unnamed x1, local copies, waits for them, and re-layouts  2.91 us

profile of v2, /device:TPU:0, one launch (start us, length us, event | category | flops | bytes accessed | tf_op | source)
XLA Modules:
  0.0 100.2 jit_solution(16984728583051869963)
XLA Ops:
  0.0 1.4 %multiply_add_fusion.ids_ref = s32[2,2048]{1,0:T(2,128)} fusion(s32[2048,2]{0,1:T(2,128)} %param.11, s32[2048,2]{0,1:T(2,128)} %param.10), kind=kLoop, calls=%fused_computation | loop fusion | flops 8192 | bytes 49152 | tf_op jit(solution)/shard_map/pair_kernels/add | solution.py:405
  1.4 69.1 %pair_kernels.1.kernel_ref = bf16[2048,512]{1,0:T(8,128)(2,1)} custom-call(bf16[512,1024]{1,0:T(8,128)(2,1)} %bitcast.11, s32[2,2048]{1,0:T(2,128)} %multiply_add_fusion.ids_ref, s32[1,2048]{1,0:T(1,128)} %bitcast.14, s32[1,2048]{1,0:T(1,128)} %bitcast.15, bf16[2048,1024]{1,0:T(8,128)(2,1)} %bitcast.10, bf16[1024,1024]{1,0:T(8,128)(2,1)} %constant.6.clone.table_hbm, ...), custom_call_target="tpu_custom_call" | custom-call | tf_op jit(solution)/shard_map/pair_kernels/pallas_call | solution.py:377
  70.4 26.9 %station_sums.1 = f32[2048,128]{1,0:T(8,128)} custom-call(s32[2,2048]{1,0:T(2,128)} %bitcast.12, s32[2,2048]{1,0:T(2,128)} %bitcast.13, bf16[2048,512]{1,0:T(8,128)(2,1)} %pair_kernels.1.kernel_ref), custom_call_target="tpu_custom_call" | custom-call | tf_op jit(solution)/shard_map/station_sums/pallas_call | solution.py:414
  97.3 2.9 %copy.11 = f32[512,1,512]{2,1,0:T(1,128)} copy(f32[512,1,512]{2,1,0:T(1,128)} %bitcast.9) | data formatting | bytes 2097152

commit v3 on v2

--- a/solution.py
+++ b/solution.py
@@ -267,9 +267,9 @@
         pl.semaphore_signal(barrier, inc=1, device_id={"pairs": peer}, device_id_type=MESH)
     pl.semaphore_wait(barrier, 3)
 
-    def partial(owner, first):
-        here = lax.broadcasted_iota(jnp.int32, (half, slot_ref.shape[1]), 0)
-        place = jnp.where(owner_ref[...] == owner, slot_ref[...] - first, -1)
+    def partial(owner):
+        here = lax.broadcasted_iota(jnp.int32, (stations, slot_ref.shape[1]), 0)
+        place = jnp.where(owner_ref[...] == owner, slot_ref[...], -1)
         hit = (here == place[0:1, :]) | (here == place[1:2, :])
         return jnp.dot(
             hit.astype(jnp.bfloat16), kernel_ref[...], preferred_element_type=jnp.float32
@@ -287,14 +287,7 @@
     sides = []
 
     def chip_sum(q, chip):
-        def other(i, carry):
-            first = pl.multiple_of(i * half, half)
-            side_send[q, pl.ds(first, half), :] = partial(chip + shift, first).astype(
-                jnp.bfloat16
-            )
-            return carry
-
-        lax.fori_loop(0, 2, other, 0)
+        side_send[q] = partial(chip + shift).astype(jnp.bfloat16)
         copy = pltpu.make_async_remote_copy(
             src_ref=side_send.at[q], dst_ref=side_recv.at[q], send_sem=side_ss.at[q],
             recv_sem=side_rs.at[q], device_id={"pairs": sibling}, device_id_type=MESH,
@@ -302,12 +295,7 @@
         copy.start()
         sides.append(copy)
 
-        def mine(i, carry):
-            first = pl.multiple_of(i * half, half)
-            sums[q, pl.ds(first, half), :] = partial(chip, first)
-            return carry
-
-        lax.fori_loop(0, 2, mine, 0)
+        sums[q] = partial(chip)
         copy.wait_recv()
 
     def whole(q, rows):
@@ -342,7 +330,7 @@
         copy.wait_recv()
     for first in (0, half):
         rows = pl.ds(first, half)
-        result = 0.25 * (
+        result = (
             whole(3, rows)
             + far_recv[0, rows, :].astype(jnp.float32)
             + far_recv[1, rows, :].astype(jnp.float32)
@@ -357,13 +345,17 @@
         copy.wait_send()
 
 
+def quarter_kernel(sums_ref, out_ref):
+    out_ref[...] = 0.25 * sums_ref[...]
+
+
 def chip_shards(spectra, observed, pair_owner, pair_slot, win_start, win_end):
     owners = lax.axis_size("pairs")
     bands = lax.axis_size("band")
     stations, _, width = spectra.shape
     half = width // 2
     pairs, _, lags = observed.shape
-    tile = min(256, pairs)
+    tile = min(512, pairs)
     bf16, f32 = jnp.bfloat16, jnp.float32
     vmem = pl.BlockSpec(memory_space=pltpu.VMEM)
     hbm = pl.BlockSpec(memory_space=pl.ANY)
@@ -431,6 +423,15 @@
                 collective_id=1, has_side_effects=True, vmem_limit_bytes=VMEM_LIMIT
             ),
         )(owner_rows, slot_rows, kernels)
+    block = pl.BlockSpec((out.shape[0] // 2, 128), lambda i: (i, 0))
+    with jax.named_scope("quarter"):
+        out = pl.pallas_call(
+            quarter_kernel,
+            out_shape=jax.ShapeDtypeStruct(out.shape, f32),
+            grid=(2,),
+            in_specs=[block],
+            out_specs=block,
+        )(out)
     return out.reshape(stations, 1, half)
 
 

time: 101 us -> 97.6 us (0.966)
  local copies, waits for them, and re-layouts: 2.91 us -> 0 us
    unnamed x1 -> x0, local copies, waits for them, and re-layouts: 2.91 us -> none
    pallas_call x0 -> x1, Pallas kernels: none -> 2.05 us  [chip_shards(): pl.pallas_call(quarter_kernel, out_shape=jax.ShapeDtypeStruct(out.shape,...]
    pallas_call x1, Pallas kernels: 69.1 us -> 67.4 us  [chip_shards(): pl.pallas_call(functools.partial(pair_kernel, bands, owners, tile), out_s...]
where the time goes in v3:
time: 97.6 us; the launch traced here: 97.3 us
  Pallas kernels  95.9 us (98%)
  other arithmetic  1.35 us (1%)
    pallas_call x1, Pallas kernels, chip_shards(): pl.pallas_call(functools.partial(pair_kernel, bands, owners, tile), out_s...  67.4 us
    pallas_call x1, Pallas kernels, chip_shards(): pl.pallas_call(functools.partial(sum_kernel, stations), out_shape=jax.Sha...  26.4 us
    pallas_call x1, Pallas kernels, chip_shards(): pl.pallas_call(quarter_kernel, out_shape=jax.ShapeDtypeStruct(out.shape,...  2.05 us

profile of v3, /device:TPU:0, one launch (start us, length us, event | category | flops | bytes accessed | tf_op | source)
XLA Modules:
  0.0 97.3 jit_solution(1492266070178705302)
XLA Ops:
  0.0 1.4 %multiply_add_fusion.ids_ref = s32[2,2048]{1,0:T(2,128)} fusion(s32[2048,2]{0,1:T(2,128)} %param.11, s32[2048,2]{0,1:T(2,128)} %param.10), kind=kLoop, calls=%fused_computation | loop fusion | flops 8192 | bytes 49152 | tf_op jit(solution)/shard_map/pair_kernels/add | solution.py:397
  1.4 67.4 %pair_kernels.1.kernel_ref = bf16[2048,512]{1,0:T(8,128)(2,1)} custom-call(bf16[512,1024]{1,0:T(8,128)(2,1)} %bitcast.10, s32[2,2048]{1,0:T(2,128)} %multiply_add_fusion.ids_ref, s32[1,2048]{1,0:T(1,128)} %bitcast.13, s32[1,2048]{1,0:T(1,128)} %bitcast.14, bf16[2048,1024]{1,0:T(8,128)(2,1)} %bitcast.9, bf16[1024,1024]{1,0:T(8,128)(2,1)} %constant.6.clone.table_hbm, ...), custom_call_target="tpu_custom_call" | custom-call | tf_op jit(solution)/shard_map/pair_kernels/pallas_call | solution.py:369
  68.8 26.4 %station_sums.1.sums_ref = f32[2048,128]{1,0:T(8,128)} custom-call(s32[2,2048]{1,0:T(2,128)} %bitcast.11, s32[2,2048]{1,0:T(2,128)} %bitcast.12, bf16[2048,512]{1,0:T(8,128)(2,1)} %pair_kernels.1.kernel_ref), custom_call_target="tpu_custom_call" | custom-call | tf_op jit(solution)/shard_map/station_sums/pallas_call | solution.py:406
  95.2 2.1 %quarter.1 = f32[2048,128]{1,0:T(8,128)} custom-call(f32[2048,128]{1,0:T(8,128)} %station_sums.1.sums_ref), custom_call_target="tpu_custom_call" | custom-call | tf_op jit(solution)/shard_map/quarter/pallas_call | solution.py:428
